TPU v7x, 256 devices: a whole 4x4x8 slice. The times are simulated.
256 devices in a mesh: seq: 8 (over y_hi, x), row: 8 (over z), col: 4 (over y_lo, core).
Axes of the slice: x: 4, y: 4 (y_hi: 2, y_lo: 2; y = y_hi * 2 + y_lo), z: 8, core: 2. Of those that a mesh axis runs over, the one named last changes fastest.
Arguments:
- alignment: int32 [32768, 256], P('seq'), may hold values from 0 to 20, as said below
- cluster_sizes: int32 [32768], P('seq'), may hold values from 1 to 32, as said below
- block_inverse: float32 [128, 128], replicated, may hold values from -12 to 12
Outputs:
- couplings: float32 [5120, 5120], P(('seq', 'row'), 'col')
Inputs may be any that keep to these rules, and one draw needn't show every extreme that they name: `alignment`: the value 20 marks a gap. `cluster_sizes`: every cluster size is a power of two.
All inputs are finite; a program needn't handle non-finite values.
Results may differ from a plain program's by a relative error of at most 0.0003.
Values sent between devices are 32-bit elements; how exact they have to be, the bound alone decides.
A program may use at most 64 MiB of HBM per device.

v0:
```python
import jax
import jax.numpy as jnp
from jax import lax
from jax.sharding import PartitionSpec as P

Q = 20
POS = 256
PANEL = 128


PSEUDOCOUNT = 0.5


def spread(value, axis, source):
    kept = jnp.where(lax.axis_index(axis) == source, value, 0).astype(value.dtype)
    return lax.psum(kept, axis)


def one_hot_states(states):
    levels = lax.broadcasted_iota(jnp.int32, (1, 1, Q), 2)
    matches = (states[:, :, None] == levels).astype(jnp.bfloat16)
    return matches.reshape(states.shape[0], states.shape[1] * Q)


def covariance_block(pair_block, row_margin, col_margin, weight_total, row_start, col_start):
    row_freq = (1.0 - PSEUDOCOUNT) * row_margin / weight_total + PSEUDOCOUNT / Q
    col_freq = (1.0 - PSEUDOCOUNT) * col_margin / weight_total + PSEUDOCOUNT / Q
    shape_rc = pair_block.shape
    row_ids = row_start + lax.broadcasted_iota(jnp.int32, shape_rc, 0)
    col_ids = col_start + lax.broadcasted_iota(jnp.int32, shape_rc, 1)
    same_pos = row_ids // Q == col_ids // Q
    prior = jnp.where(
        same_pos, jnp.where(row_ids == col_ids, PSEUDOCOUNT / Q, 0.0), PSEUDOCOUNT / (Q * Q)
    )
    joint = (1.0 - PSEUDOCOUNT) * pair_block / weight_total + prior
    return joint - row_freq[:, None] * col_freq[None, :]


def accumulate_pairs(row_states, column_sets, span_widths, seq_weight):
    local_seqs = row_states.shape[0]
    block_rows = min(local_seqs, 1024)
    count_blocks = local_seqs // block_rows
    row_width = row_states.shape[1] * Q

    def blocked(states):
        return states.reshape(count_blocks, block_rows, states.shape[1])

    def add_block(running, block_item):
        pair_totals, row_margin, column_margins = running
        row_block, weight_block, column_blocks = block_item
        row_hot = one_hot_states(row_block)
        weighted = row_hot * weight_block[:, None]
        new_pairs = []
        new_margins = []
        for pair_total, margin_total, states_block, span_width in zip(
            pair_totals, column_margins, column_blocks, span_widths
        ):
            column_hot = one_hot_states(states_block)
            new_pairs.append(
                pair_total
                + lax.dot_general(
                    weighted,
                    column_hot,
                    (((0,), (0,)), ((), ())),
                    preferred_element_type=jnp.float32,
                )
            )
            new_margins.append(
                margin_total + jnp.dot(weight_block, column_hot, preferred_element_type=jnp.float32)
            )
        row_margin = row_margin + jnp.dot(weight_block, row_hot, preferred_element_type=jnp.float32)
        return ((tuple(new_pairs), row_margin, tuple(new_margins)), None)

    initial = (
        tuple((jnp.zeros((row_width, span_width), jnp.float32) for span_width in span_widths)),
        jnp.zeros((row_width,), jnp.float32),
        tuple((jnp.zeros((span_width,), jnp.float32) for span_width in span_widths)),
    )
    block_items = (
        blocked(row_states),
        seq_weight.reshape(count_blocks, block_rows),
        tuple((blocked(states) for states in column_sets)),
    )
    result, unused = lax.scan(add_block, initial, block_items)
    return result


def shards(alignment, cluster_sizes, block_inverse):
    seq_count = lax.axis_size("seq")
    row_count = lax.axis_size("row")
    col_count = lax.axis_size("col")
    seq_index = lax.axis_index("seq")
    row_index = lax.axis_index("row")
    col_index = lax.axis_index("col")
    local_seqs = alignment.shape[0]
    row_positions = POS // (seq_count * row_count)
    col_positions = POS // col_count
    block_features = row_positions * Q
    col_features = col_positions * Q
    seq_weight = (1.0 / cluster_sizes.astype(jnp.float32)).astype(jnp.bfloat16)
    grouped = alignment.reshape(local_seqs, seq_count, row_count, row_positions)
    row_states = lax.dynamic_slice_in_dim(grouped, row_index, 1, 2).reshape(
        local_seqs, seq_count * row_positions
    )
    col_states = lax.dynamic_slice_in_dim(alignment, col_index * col_positions, col_positions, 1)
    weight_local = jnp.sum(seq_weight.astype(jnp.float32))
    row_start = (seq_index * row_count + row_index) * block_features
    col_start = col_index * col_features
    pair_totals, row_margin, column_margins = accumulate_pairs(
        row_states, (col_states,), (col_features,), seq_weight
    )
    weight_total, row_margin, col_margin = lax.psum(
        (weight_local, row_margin, column_margins[0]), "seq"
    )
    pair_tile = lax.psum_scatter(pair_totals[0], "seq", scatter_dimension=0, tiled=True)
    own_margin = lax.dynamic_slice_in_dim(row_margin, seq_index * block_features, block_features)
    cov_tile = covariance_block(
        pair_tile, own_margin, col_margin, weight_total, row_start, col_start
    )
    panel_rows = spread(cov_tile[:, :PANEL], "col", 0)
    sym_inverse = 0.5 * (block_inverse + block_inverse.T)
    left_factor = jnp.dot(panel_rows, sym_inverse, precision=lax.Precision.HIGHEST)
    whole_panel = lax.all_gather(panel_rows, ("seq", "row"), axis=0, tiled=True)
    panel_cols = lax.dynamic_slice_in_dim(whole_panel, col_start, col_features, 0)
    update = lax.dot_general(
        left_factor, panel_cols, (((1,), (1,)), ((), ())), precision=lax.Precision.HIGHEST
    )
    return -Q * (cov_tile - update)


def solution(mesh):
    in_specs = (P("seq", None), P("seq"), P())
    out_specs = P(("seq", "row"), "col")
    return jax.shard_map(shards, mesh=mesh, in_specs=in_specs, out_specs=out_specs, check_vma=False)
```

profile of v0, /device:TPU:6, one launch (start us, length us, event | category | flops | bytes accessed | tf_op | source)
XLA Modules:
  0.0 306.2 jit_solution(9124577262664192869)
XLA Ops:
  6.5 5.6 %copy.9 = s32[4096,256]{0,1:T(8,128)} copy(s32[4096,256]{1,0:T(8,128)} %param.5) | data formatting | bytes 8388608 | tf_op args[0]
  12.1 2.2 constant_dynamic-slice_fusion.4
  14.3 0.6 copy.12
  14.9 5.2 %reshape.159 = s32[4096,8,8,4]{0,3,2,1:T(4,128)} reshape(s32[4096,256]{0,1:T(8,128)} %copy.9) | data formatting | bytes 8388608 | tf_op jit(solution)/shard_map/reshape | solution.py:101
  20.1 1.1 constant_dynamic-slice_fusion.5
  21.2 1.2 reshape_reshape.3
  22.5 0.7 convert_reduce_fusion
  23.1 51.7 %while.15 = (s32[]{:T(128)}, f32[640,1280]{1,0:T(8,128)}, f32[640]{0:T(1024)S(1)}, f32[1280]{0:T(1024)S(1)}, s32[4,1024,32]{1,0,2:T(4,128)}, /*index=5*/bf16[4,1...) while((s32[]{:T(128)}, f32[640,1280]{1,0:T(8,128)}, f32[640]{0:T(1024)S(1)}, ...), condition=%wide.region_1.2_spmd.clone, body=%wide.region_0.0_spmd.clone.sunk | while | flops 1686572800 | bytes 30978228 | solution.py:84
  23.2 1.5 constant_dynamic-slice_fusion.7
  24.8 0.5 broadcast_select_fusion.2
  25.2 1.2 mul.117
  26.5 0.9 iota_compare_fusion.4
  27.4 0.7 eq.120
  28.2 5.0 %convolution_add_fusion.2 = f32[640,1280]{1,0:T(8,128)} fusion(bf16[1024,640]{0,1:T(8,128)(2,1)} %mul.117, pred[1024,1280]{0,1:T(32,128)(4,1)S(1)} %eq.120, f32[640,1280]{1,0:T(8,128)} %get-tuple-element.161, pred[]{:T(512)S(6)} %compare.3), kind=kOutput, calls=%fused_computation.1.clone.1 | convolution fusion | flops 1679360000 | bytes 9175041 | tf_op jit(solution)/shard_map/while/body/eval_jaxpr/dot_general | solution.py:61
  33.2 0.8 convolution_reduce_fusion.5
  34.0 0.4 iota_compare_fusion.5
  34.4 0.4 eq.121
  34.8 0.5 convolution_reduce_fusion.4
  35.3 0.0 copy-done.1
  35.4 1.5 constant_dynamic-slice_fusion.7
  36.9 0.5 broadcast_select_fusion.2
  37.4 1.2 mul.117
  38.7 0.9 iota_compare_fusion.4
  39.6 0.7 eq.120
  40.3 6.0 %convolution_add_fusion.2 = f32[640,1280]{1,0:T(8,128)} fusion(bf16[1024,640]{0,1:T(8,128)(2,1)} %mul.117, pred[1024,1280]{0,1:T(32,128)(4,1)S(1)} %eq.120, f32[640,1280]{1,0:T(8,128)} %get-tuple-element.161, pred[]{:T(512)S(6)} %compare.3), kind=kOutput, calls=%fused_computation.1.clone.1 | convolution fusion | flops 1679360000 | bytes 9175041 | tf_op jit(solution)/shard_map/while/body/eval_jaxpr/dot_general | solution.py:61
  46.4 0.8 convolution_reduce_fusion.5
  47.2 0.4 iota_compare_fusion.5
  47.6 0.4 eq.121
  48.0 0.5 convolution_reduce_fusion.4
  48.5 1.5 constant_dynamic-slice_fusion.7
  50.1 0.5 broadcast_select_fusion.2
  50.6 1.2 mul.117
  51.8 0.9 iota_compare_fusion.4
  52.8 0.7 eq.120
  53.5 6.0 %convolution_add_fusion.2 = f32[640,1280]{1,0:T(8,128)} fusion(bf16[1024,640]{0,1:T(8,128)(2,1)} %mul.117, pred[1024,1280]{0,1:T(32,128)(4,1)S(1)} %eq.120, f32[640,1280]{1,0:T(8,128)} %get-tuple-element.161, pred[]{:T(512)S(6)} %compare.3), kind=kOutput, calls=%fused_computation.1.clone.1 | convolution fusion | flops 1679360000 | bytes 9175041 | tf_op jit(solution)/shard_map/while/body/eval_jaxpr/dot_general | solution.py:61
  59.6 0.8 convolution_reduce_fusion.5
  60.4 0.4 iota_compare_fusion.5
  60.8 0.4 eq.121
  61.2 0.5 convolution_reduce_fusion.4
  61.7 0.0 copy-done.1
  61.7 1.5 constant_dynamic-slice_fusion.7
  63.3 0.5 broadcast_select_fusion.2
  63.8 1.2 mul.117
  65.0 0.9 iota_compare_fusion.4
  66.0 0.7 eq.120
  66.7 6.0 %convolution_add_fusion.2 = f32[640,1280]{1,0:T(8,128)} fusion(bf16[1024,640]{0,1:T(8,128)(2,1)} %mul.117, pred[1024,1280]{0,1:T(32,128)(4,1)S(1)} %eq.120, f32[640,1280]{1,0:T(8,128)} %get-tuple-element.161, pred[]{:T(512)S(6)} %compare.3), kind=kOutput, calls=%fused_computation.1.clone.1 | convolution fusion | flops 1679360000 | bytes 9175041 | tf_op jit(solution)/shard_map/while/body/eval_jaxpr/dot_general | solution.py:61
  72.8 0.8 convolution_reduce_fusion.5
  73.6 0.4 iota_compare_fusion.5
  74.0 0.4 eq.121
  74.4 0.5 convolution_reduce_fusion.4
  74.9 0.0 copy-start.2
  74.9 0.0 reduce-scatter.2.cloned.1.call-update
  74.9 0.0 all-gather.2.cloned.1.call-start
  75.0 36.3 %all-reduce = (f32[1280]{0:T(1024)S(1)}, f32[]{:T(128)}, f32[640]{0:T(1024)S(1)}) all-reduce(f32[1280]{0:T(1024)S(1)} %get-tuple-element.46, f32[]{:T(128)} %get-tuple-element.102, f32[640]{0:T(1024)S(1)} %get-tuple-element.45), channel_id=1, replica_groups=mesh['seq'=8,'row'=8,'col'=4] {'seq'}, use_global_device_ids=true, to_apply=%region_6.7 | all-reduce | flops 1921 | bytes 15368 | tf_op jit(solution)/shard_map/psum | solution.py:112
  111.3 0.7 divide_add_fusion.1
  112.1 0.7 divide_add_fusion
  112.7 51.2 %reduce-scatter.2.cloned.1.call-done = f32[80,1280]{1,0:T(8,128)} async-done(((f32[640,1280]{1,0:T(8,128)}), f32[80,1280]{1,0:T(8,128)}) %reduce-scatter.2.cloned.1.call-update) | async-done | bytes 409616 | tf_op jit(solution)/shard_map/reduce_scatter | solution.py:115
  163.9 1.8 multiply_subtract_fusion
  165.8 11.4 %psum.31 = f32[80,128]{1,0:T(8,128)} all-reduce(f32[80,128]{1,0:T(8,128)S(1)} %slice_select_fusion), channel_id=1, replica_groups=mesh['seq'=8,'row'=8,'col'=4] {'col'}, use_global_device_ids=true, to_apply=%region_7.8 | all-reduce | flops 10240 | bytes 81920 | tf_op jit(solution)/shard_map/psum | solution.py:16
  177.2 0.0 all-gather.2.cloned.1.call-update
  177.2 0.1 copy.13
  177.3 1.0 fusion.6
  178.3 118.5 %all-gather.2.cloned.1.call-done = f32[5120,128]{1,0:T(8,128)} async-done(((f32[80,128]{1,0:T(8,128)}), f32[5120,128]{1,0:T(8,128)}) %all-gather.2.cloned.1.call-update) | async-done | bytes 2621456 | tf_op jit(solution)/shard_map/all_gather | solution.py:123
  296.8 2.6 fusion.3
  (49 shorter events, 0.5 us)
Async XLA Ops:
  6.5 157.4 %reduce-scatter.2.cloned.1.call-start = ((), (), s32[]{:S(2)}) async-start(), calls=%async_computation.1 | async-start | bytes 3686400 | tf_op jit(solution)/shard_map/reduce_scatter | solution.py:115
  20.1 2.3 copy-start.3
  23.1 3.3 %copy-start = (s32[4,1024,64]{1,2,0:T(8,128)}, s32[4,1024,64]{1,2,0:T(8,128)S(1)}, u32[]{:S(2)}) copy-start(s32[4,1024,64]{1,2,0:T(8,128)S(1)} %get-tuple-element.175) | copy-start | bytes 3145732 | tf_op jit(solution)/shard_map/while
  33.2 2.1 copy-start.1
  35.3 3.3 %copy-start = (s32[4,1024,64]{1,2,0:T(8,128)}, s32[4,1024,64]{1,2,0:T(8,128)S(1)}, u32[]{:S(2)}) copy-start(s32[4,1024,64]{1,2,0:T(8,128)S(1)} %get-tuple-element.175) | copy-start | bytes 3145732 | tf_op jit(solution)/shard_map/while
  46.4 2.1 copy-start.1
  48.5 3.3 %copy-start = (s32[4,1024,64]{1,2,0:T(8,128)}, s32[4,1024,64]{1,2,0:T(8,128)S(1)}, u32[]{:S(2)}) copy-start(s32[4,1024,64]{1,2,0:T(8,128)S(1)} %get-tuple-element.175) | copy-start | bytes 3145732 | tf_op jit(solution)/shard_map/while
  59.6 2.1 copy-start.1
  61.7 3.3 %copy-start = (s32[4,1024,64]{1,2,0:T(8,128)}, s32[4,1024,64]{1,2,0:T(8,128)S(1)}, u32[]{:S(2)}) copy-start(s32[4,1024,64]{1,2,0:T(8,128)S(1)} %get-tuple-element.175) | copy-start | bytes 3145732 | tf_op jit(solution)/shard_map/while
  72.8 2.1 copy-start.1
  74.9 102.3 %copy-start.2 = (f32[128,128]{1,0:T(8,128)S(1)}, f32[128,128]{1,0:T(8,128)}, u32[]{:S(2)}) copy-start(f32[128,128]{1,0:T(8,128)} %param.7) | copy-start | bytes 196612
  74.9 221.8 %all-gather.2.cloned.1.call-start = ((), (), s32[]{:S(2)}) async-start(), calls=%async_computation.2 | async-start | bytes 2662400 | tf_op jit(solution)/shard_map/all_gather | solution.py:123
Sparse Core Ops, SparseCore 0:
  75.0 88.8 reduce-scatter.1
  177.3 119.4 all-gather.1
where the time goes:
time: 307 us; the launch traced here: 306 us
  waiting for transfers between devices  170 us (55%)
  blocking collectives  47.6 us (16%)
  matrix products  31.8 us (10%)
  local copies, waits for them, and re-layouts  31.7 us (10%)
  between operations  13.5 us (4%)
  other arithmetic  11.4 us (4%)
    all_gather x1, waiting for transfers between devices, shards(): whole_panel = lax.all_gather(panel_rows, ('seq', 'row'), axis=0, tiled=True)  118 us
    reduce_scatter x1, waiting for transfers between devices, shards(): lax.psum_scatter(pair_totals[0], 'seq', scatter_dimension=0, tiled=True)  51.2 us
    psum x1, blocking collectives, shards(): lax.psum((weight_local, row_margin, column_margins[0]), 'seq')  36.3 us
    dot_general x4, matrix products, add_block(): lax.dot_general(weighted, column_hot, (((0,), (0,)), ((), ())), preferred...  23.1 us
    psum x1, blocking collectives, spread(): return lax.psum(kept, axis)  11.4 us
    dynamic_slice x12, local copies, waits for them, and re-layouts, accumulate_pairs(): result, unused = lax.scan(add_block, initial, block_items)  6.38 us
    unnamed x7, local copies, waits for them, and re-layouts  6.29 us
  transfers between devices with their start and end apart: 2, of which 2 were waited for; matrix products, arithmetic and copies ran while one was open for 1% of the time, Pallas kernels for 0%

commit v1 on v0

v1 whole, which is shorter than its diff:
```python
import jax
import jax.numpy as jnp
from jax import lax
from jax.experimental import pallas as pl
from jax.experimental.pallas import tpu as pltpu
from jax.sharding import PartitionSpec as P

Q = 20
POS = 256
PANEL = 128
SEQS_LOCAL = 4096
ROWS = 80
COLS = 1280
CHUNK = 256
CHUNKS = COLS // CHUNK
MAIN = 640
LEFT = 672
LOAD = 512
LANES = 128
HOT = jnp.float8_e4m3fn
F32 = jnp.float32
MESH = pl.DeviceIdType.MESH
X_FIRST = (True, False, True, False, True)
N_COPIES = 80
HIGHEST = lax.Precision.HIGHEST
CONTRACT_LAST = (((1,), (1,)), ((), ()))


def position_of(feature):
    return (feature * 3277) >> 16


def hot_rows(state_row, value):
    lanes = LANES
    row = lax.broadcasted_iota(jnp.int32, (8, lanes), 0).astype(F32)
    parts = []
    for tile in range(Q):
        low = 8 * tile
        first, last = low // Q, (low + 7) // Q
        base = float(low - Q * first)
        states = jnp.broadcast_to(state_row(first), (8, lanes))
        level = row + base
        if last != first:
            cut = float(Q * last - low)
            before = row < cut
            states = jnp.where(before, states, jnp.broadcast_to(state_row(last), (8, lanes)))
            level = jnp.where(before, level, row - cut)
        parts.append(jnp.where(states == level, value, 0.0))
    return jnp.concatenate(parts, 0)


def kernel(
    align_hbm, sizes_ref, inverse_ref, out_ref,
    align, states, left, right, pairs, xr, yr, yr4, final, eu, er, es, eg, zg, mc, pr, panel_t,
    load_sem, send_sem, recv_sem,
):
    s = lax.axis_index("seq")
    r = lax.axis_index("row")
    c = lax.axis_index("col")
    yh, x = s // 4, s % 4
    x_next, x_far, x_prev = (x + 1) % 4, (x + 2) % 4, (x + 3) % 4
    loads = []
    for i in range(SEQS_LOCAL // LOAD):
        rows = pl.ds(i * LOAD, LOAD)
        copy = pltpu.make_async_copy(align_hbm.at[rows, :], align.at[rows, :], load_sem.at[i])
        copy.start()
        loads.append(copy)

    def seq_of(to_yh, to_x):
        return to_yh * 4 + to_x

    def at_seq(dx, dy):
        return (seq_of((yh + dy) % 2, (x + dx) % 4), r, c)

    barrier = pltpu.get_barrier_semaphore()
    peers = [at_seq(dx, dy) for dx in range(4) for dy in range(2) if dx or dy]
    peers += [(s, (r + dz) % 8, c) for dz in range(1, 8)]
    peers += [(s, r, (c + dc) % 4) for dc in range(1, 4)]
    for peer in peers:
        pl.semaphore_signal(barrier, inc=1, device_id=peer, device_id_type=MESH)

    used = []
    sends = []

    def push(src, dst, device):
        index = len(used)
        used.append(index)
        copy = pltpu.make_async_remote_copy(
            src_ref=src, dst_ref=dst, send_sem=send_sem.at[index], recv_sem=recv_sem.at[index],
            device_id=device, device_id_type=MESH,
        )
        copy.start()
        sends.append(copy)
        return copy

    row_id = lax.broadcasted_iota(jnp.int32, (112, POS), 0)
    pos_id = lax.broadcasted_iota(jnp.int32, (112, POS), 1)
    wanted = jnp.where(
        row_id < 32,
        (row_id >> 2) * 32 + r * 4 + (row_id & 3),
        jnp.where(row_id < 96, c * 64 + row_id - 32, position_of(r * 16 + row_id - 96)),
    )
    pick = (pos_id == wanted).astype(F32).astype(jnp.bfloat16)
    for i in range(SEQS_LOCAL // LOAD):
        loads[i].wait()
        block = align[pl.ds(i * LOAD, LOAD), :].astype(F32).astype(jnp.bfloat16)
        states[:, pl.ds(i * LOAD, LOAD)] = lax.dot_general(
            pick, block, CONTRACT_LAST, preferred_element_type=F32
        )

    feature = r * 16 + lax.broadcasted_iota(jnp.int32, (16, LANES), 0)
    panel_level = (feature - position_of(feature) * Q).astype(F32)
    first_row = lax.broadcasted_iota(jnp.int32, (16, LANES), 0) == 0

    @pl.loop(0, SEQS_LOCAL // LANES)
    def _(i):
        lanes = pl.ds(pl.multiple_of(i * LANES, LANES), LANES)
        weight = 1.0 / sizes_ref[pl.ds(i, 1), :].astype(F32)
        weight8 = jnp.broadcast_to(weight, (8, LANES))
        weight16 = jnp.broadcast_to(weight, (16, LANES))
        for b in range(4):
            left[pl.ds(160 * b, 160), lanes] = hot_rows(
                lambda p: states[pl.ds(b * 8 + p, 1), lanes], weight8
            ).astype(HOT)
        panel_hot = jnp.where(states[pl.ds(96, 16), lanes] == panel_level, weight16, 0.0)
        weight_row = jnp.where(first_row, weight16, 0.0)
        left[pl.ds(MAIN, 32), lanes] = jnp.concatenate([panel_hot, weight_row], 0).astype(HOT)
        for b in range(8):
            right[pl.ds(160 * b, 160), lanes] = hot_rows(
                lambda p: states[pl.ds(32 + b * 8 + p, 1), lanes], 1.0
            ).astype(HOT)

    def multiply(j):
        pairs[j] = lax.dot_general(
            left[...], right[pl.ds(j * CHUNK, CHUNK), :], CONTRACT_LAST, preferred_element_type=F32
        )

    def block(j, to_yh, to_x, low=0, size=ROWS):
        start = pl.multiple_of(seq_of(to_yh, to_x) * ROWS + low, 8)
        return pairs.at[j, pl.ds(start, size), :]

    copies = {}

    def stage_one(j):
        if X_FIRST[j]:
            k = X_FIRST[:j].count(True)
            copies[j] = [
                push(block(j, 0, x_far), xr.at[k, 0], at_seq(1, 0)),
                push(block(j, 1, x_far), xr.at[k, 1], at_seq(3, 0)),
                push(block(j, 1, x_next), xr.at[k, 2], at_seq(1, 0)),
                push(block(j, 0, x_prev), xr.at[k, 3], at_seq(3, 0)),
            ]
        else:
            k = X_FIRST[:j].count(False)
            copies[j] = [
                push(block(j, 1 - yh, to_x), yr4.at[k, i], at_seq(0, 1))
                for i, to_x in enumerate((x_far, x_next, x_prev, x))
            ]

    def stage_two(j):
        done = copies[j]
        if X_FIRST[j]:
            k = X_FIRST[:j].count(True)
            done[0].wait_recv()
            target = block(j, 0, x_next)
            target[...] += xr[k, 0]
            done.append(push(target, xr.at[k, 4], at_seq(1, 0)))
            done[1].wait_recv()
            target = block(j, 1, x_prev)
            target[...] += xr[k, 1]
            done.append(push(target, xr.at[k, 5], at_seq(3, 0)))
        else:
            k = X_FIRST[:j].count(False)
            done[0].wait_recv()
            yr4[k, 0] += block(j, yh, x_far)[...]
            done.append(push(yr4.at[k, 0, pl.ds(0, 40), :], yr.at[k, 0], at_seq(1, 0)))
            done.append(push(yr4.at[k, 0, pl.ds(40, 40), :], yr.at[k, 1], at_seq(3, 0)))
            done[1].wait_recv()
            yr4[k, 1] += block(j, yh, x_next)[...]
            done.append(push(yr4.at[k, 1, pl.ds(40, 40), :], yr.at[k, 2], at_seq(1, 0)))
            done[2].wait_recv()
            yr4[k, 2] += block(j, yh, x_prev)[...]
            done.append(push(yr4.at[k, 2, pl.ds(0, 40), :], yr.at[k, 3], at_seq(3, 0)))

    def stage_three(j):
        done = copies[j]
        if X_FIRST[j]:
            k = X_FIRST[:j].count(True)
            for i in range(2, 6):
                done[i].wait_recv()
            mine = block(j, 0, x)
            mine[...] += xr[k, 4] + xr[k, 3]
            mine = block(j, 1, x)
            mine[...] += xr[k, 2] + xr[k, 5]
            done.append(push(block(j, 1 - yh, x), xr.at[k, 6], at_seq(0, 1)))
        else:
            k = X_FIRST[:j].count(False)
            done[4].wait_recv()
            yr4[k, 1, pl.ds(0, 40), :] += yr[k, 0]
            done.append(push(yr4.at[k, 1, pl.ds(0, 40), :], yr.at[k, 4], at_seq(1, 0)))
            done[5].wait_recv()
            yr4[k, 2, pl.ds(40, 40), :] += yr[k, 1]
            done.append(push(yr4.at[k, 2, pl.ds(40, 40), :], yr.at[k, 5], at_seq(3, 0)))

    def finish(j):
        done = copies[j]
        if X_FIRST[j]:
            k = X_FIRST[:j].count(True)
            done[6].wait_recv()
            final[j] = block(j, yh, x)[...] + xr[k, 6]
        else:
            k = X_FIRST[:j].count(False)
            for i in (3, 6, 7, 8, 9):
                done[i].wait_recv()
            own = block(j, yh, x)
            final[j, pl.ds(0, 40), :] = (
                own[pl.ds(0, 40), :] + yr4[k, 3, pl.ds(0, 40), :] + yr[k, 4] + yr[k, 3]
            )
            final[j, pl.ds(40, 40), :] = (
                own[pl.ds(40, 40), :] + yr4[k, 3, pl.ds(40, 40), :] + yr[k, 2] + yr[k, 5]
            )

    def lane_tile(tile):
        return tile // 2, pl.ds((tile % 2) * LANES, LANES)

    multiply(0)
    pl.semaphore_wait(barrier, len(peers))
    stage_one(0)
    multiply(1)
    stage_one(1)
    multiply(2)
    stage_one(2)
    stage_two(0)
    multiply(3)
    stage_one(3)
    stage_two(1)
    multiply(4)

    weight_sum = jnp.sum(
        jnp.sum(1.0 / sizes_ref[...].astype(F32), axis=0, keepdims=True), axis=1, keepdims=True
    )
    for u in range(4):
        g, h = u // 2, u % 2
        for t in range(5):
            j, lanes = lane_tile(h * 5 + t)
            eu[u, pl.ds(8 * t, 8), :] = pairs[j, pl.ds(MAIN + 8 * g, 8), lanes]
        for tile in range(10):
            j, lanes = lane_tile(tile)
            eu[u, pl.ds(40 + tile, 1), :] = pairs[j, pl.ds(MAIN + 16, 1), lanes]
        eu[u, pl.ds(50, 6), :] = jnp.broadcast_to(weight_sum, (6, LANES))
    panel_sums = []
    for dx in range(4):
        for dy in range(2):
            if dx or dy:
                panel_sums.append(
                    push(eu.at[(x + dx) % 4], er.at[dx * 2 + dy - 1], at_seq(dx, dy))
                )
    stage_one(4)
    stage_two(2)
    stage_three(0)
    for copy in panel_sums:
        copy.wait_recv()
    total = eu[x]
    for i in range(7):
        total = total + er[i]
    eg[x] = total[0:40]
    mc[c] = total[40:56]
    es[...] = total
    panel_gathers = [
        push(es.at[pl.ds(0, 40), :], eg.at[x], at_seq(dx, 0)) for dx in range(1, 4)
    ]
    margin_gathers = [
        push(es.at[pl.ds(40, 16), :], mc.at[c], (s, r, (c + dc) % 4)) for dc in range(1, 4)
    ]
    stage_two(3)
    stage_three(1)
    for copy in panel_gathers:
        copy.wait_recv()
    zg[r] = eg[...]
    z_gathers = [push(eg, zg.at[r], (s, (r + dz) % 8, c)) for dz in range(1, 8)]
    finish(0)
    row_index = [len(used) + i for i in range(3)]
    used.extend(row_index)

    def row_copy(i):
        return pltpu.make_async_remote_copy(
            src_ref=final.at[0, :, pl.ds(0, PANEL)], dst_ref=pr,
            send_sem=send_sem.at[row_index[i]], recv_sem=recv_sem.at[row_index[0]],
            device_id=(s, r, (c + 1 + i) % 4), device_id_type=MESH,
        )

    @pl.when(c == 0)
    def _():
        for i in range(3):
            row_copy(i).start()
        pr[...] = final[0, :, pl.ds(0, PANEL)]

    stage_two(4)
    stage_three(2)
    stage_three(3)
    finish(1)
    stage_three(4)
    finish(2)
    finish(3)

    @pl.when(c != 0)
    def _():
        row_copy(0).wait_recv()

    for copy in margin_gathers:
        copy.wait_recv()
    half = 0.5 / mc[c, pl.ds(10, 1), :]
    floor = 0.5 / Q
    half_cols = jnp.concatenate([half] * 10, 1)
    col_freq = (
        jnp.concatenate([mc[c, pl.ds(i, 1), :] for i in range(10)], 1) * half_cols + floor
    )
    panel_freq = mc[0, pl.ds(0, 1), :] * half + floor
    row_low = (s * 8 + r) * ROWS
    local = (s % 2) * MAIN + r * ROWS + lax.broadcasted_iota(jnp.int32, (ROWS, LANES), 0)
    lane = lax.broadcasted_iota(jnp.int32, (ROWS, LANES), 1)
    found = jnp.zeros((ROWS, LANES), F32)
    for i in range(10):
        found += jnp.where(
            local == lane + i * LANES, jnp.broadcast_to(mc[s // 2, pl.ds(i, 1), :] * half, (ROWS, LANES)), 0.0
        )
    row_freq = jnp.sum(found, axis=1, keepdims=True) + floor
    eye = lax.broadcasted_iota(jnp.int32, (PANEL, PANEL), 0) == lax.broadcasted_iota(
        jnp.int32, (PANEL, PANEL), 1
    )
    panel_freq_column = jnp.sum(
        jnp.where(eye, jnp.broadcast_to(panel_freq, (PANEL, PANEL)), 0.0), axis=1, keepdims=True
    )

    def covariance(sums, scale, freq_rows, freq_cols, first, col_first):
        shape = sums.shape
        row = first + lax.broadcasted_iota(jnp.int32, shape, 0)
        col = col_first + lax.broadcasted_iota(jnp.int32, shape, 1)
        prior = jnp.where(
            position_of(row) == position_of(col),
            jnp.where(row == col, 0.5 / Q, 0.0),
            0.5 / (Q * Q),
        )
        return sums * scale + prior - freq_rows * freq_cols

    panel_rows = covariance(pr[...], half, row_freq, panel_freq, row_low, 0)
    symmetric = 0.5 * (inverse_ref[...] + inverse_ref[...].T)
    factor = jnp.dot(panel_rows, symmetric, precision=HIGHEST, preferred_element_type=F32)
    for copy in z_gathers:
        copy.wait_recv()
    for tile in range(10):
        h, t = tile // 5, tile % 5
        for k in range(16):
            panel_t[tile // 2, pl.ds(8 * k, 8), pl.ds((tile % 2) * LANES, LANES)] = zg[
                k // 2, (k % 2) * 2 + h, pl.ds(8 * t, 8), :
            ]
    for j in range(CHUNKS):
        if j == CHUNKS - 1:
            finish(4)
        columns = pl.ds(j * CHUNK, CHUNK)
        scale = half_cols[:, j * CHUNK:(j + 1) * CHUNK]
        freq = col_freq[:, j * CHUNK:(j + 1) * CHUNK]
        col_low = c * COLS + j * CHUNK
        panel_cols = covariance(panel_t[j], scale, panel_freq_column, freq, 0, col_low)
        update = jnp.dot(factor, panel_cols, precision=HIGHEST, preferred_element_type=F32)
        cov = covariance(final[j], scale, row_freq, freq, row_low, col_low)
        out_ref[:, columns] = -float(Q) * (cov - update)

    for copy in sends:
        copy.wait_send()

    @pl.when(c == 0)
    def _():
        for i in range(3):
            row_copy(i).wait_send()

    assert len(used) <= N_COPIES


def shards(alignment, cluster_sizes, block_inverse):
    x_chunks = X_FIRST.count(True)
    y_chunks = X_FIRST.count(False)
    vmem = pl.BlockSpec(memory_space=pltpu.VMEM)
    return pl.pallas_call(
        kernel,
        out_shape=jax.ShapeDtypeStruct((ROWS, COLS), F32),
        in_specs=[pl.BlockSpec(memory_space=pl.ANY), vmem, vmem],
        out_specs=vmem,
        scratch_shapes=[
            pltpu.VMEM((SEQS_LOCAL, POS), jnp.int32),
            pltpu.VMEM((112, SEQS_LOCAL), F32),
            pltpu.VMEM((LEFT, SEQS_LOCAL), HOT),
            pltpu.VMEM((COLS, SEQS_LOCAL), HOT),
            pltpu.VMEM((CHUNKS, LEFT, CHUNK), F32),
            pltpu.VMEM((x_chunks, 7, ROWS, CHUNK), F32),
            pltpu.VMEM((y_chunks, 6, 40, CHUNK), F32),
            pltpu.VMEM((y_chunks, 4, ROWS, CHUNK), F32),
            pltpu.VMEM((CHUNKS, ROWS, CHUNK), F32),
            pltpu.VMEM((4, 56, LANES), F32),
            pltpu.VMEM((7, 56, LANES), F32),
            pltpu.VMEM((56, LANES), F32),
            pltpu.VMEM((4, 40, LANES), F32),
            pltpu.VMEM((8, 4, 40, LANES), F32),
            pltpu.VMEM((4, 16, LANES), F32),
            pltpu.VMEM((ROWS, PANEL), F32),
            pltpu.VMEM((CHUNKS, PANEL, CHUNK), F32),
            pltpu.SemaphoreType.DMA((SEQS_LOCAL // LOAD,)),
            pltpu.SemaphoreType.DMA((N_COPIES,)),
            pltpu.SemaphoreType.DMA((N_COPIES,)),
        ],
        compiler_params=pltpu.CompilerParams(
            collective_id=0, has_side_effects=True, vmem_limit_bytes=56 * 2**20
        ),
        name="couplings",
    )(alignment, cluster_sizes.reshape(SEQS_LOCAL // LANES, LANES), block_inverse)


def solution(mesh):
    in_specs = (P("seq", None), P("seq"), P())
    out_specs = P(("seq", "row"), "col")
    return jax.shard_map(shards, mesh=mesh, in_specs=in_specs, out_specs=out_specs, check_vma=False)
```

time: 307 us -> 60.3 us (0.20)
  waiting for transfers between devices: 170 us -> 0 us
  Pallas kernels: 0 us -> 57.5 us
  blocking collectives: 47.6 us -> 0 us
  matrix products: 31.8 us -> 0 us
  local copies, waits for them, and re-layouts: 31.7 us -> 1.78 us
  between operations: 13.5 us -> 0.01 us
  other arithmetic: 11.4 us -> 0 us
    all_gather x1 -> x0, waiting for transfers between devices: 118 us -> none  [shards(): whole_panel = lax.all_gather(panel_rows, ('seq', 'row'), axis=0, tiled=True)]
    pallas_call x0 -> x1, Pallas kernels: none -> 57.5 us  [shards(): pl.pallas_call(kernel, out_shape=jax.ShapeDtypeStruct((ROWS, COLS), F32),...]
    reduce_scatter x1 -> x0, waiting for transfers between devices: 51.2 us -> none  [shards(): lax.psum_scatter(pair_totals[0], 'seq', scatter_dimension=0, tiled=True)]
    psum x2 -> x0, blocking collectives: 47.6 us -> none  [the longest x1 36.3 us: shards(): lax.psum((weight_local, row_margin, column_margins[0]), 'seq')]
    dot_general x14 -> x0, matrix products: 31.8 us -> none  [the longest x4 23.1 us: add_block(): lax.dot_general(weighted, column_hot, (((0,), (0,)), ((), ())), preferred...]
    dynamic_slice x14 -> x0, local copies, waits for them, and re-layouts: 9.66 us -> none  [the longest x12 6.38 us: accumulate_pairs(): result, unused = lax.scan(add_block, initial, block_items)]
    eq x8 -> x0, other arithmetic: 5.45 us -> none  [one_hot_states(): matches = (states[:, :, None] == levels).astype(jnp.bfloat16)]
    reshape x2 -> x0, local copies, waits for them, and re-layouts: 5.18 us -> none  [the longest x1 5.17 us: shards(): grouped = alignment.reshape(local_seqs, seq_count, row_count, row_positions)]
  transfers between devices with their start and end apart: 2 -> 0, of which waited for: 2 -> 0; matrix products, arithmetic and copies ran while one was open for 1% -> 0% of each run, Pallas kernels for 0% -> 0%
where the time goes in v1:
time: 60.3 us; the launch traced here: 59.3 us
  Pallas kernels  57.5 us (95%)
  local copies, waits for them, and re-layouts  1.78 us (3%)
    pallas_call x1, Pallas kernels, shards(): pl.pallas_call(kernel, out_shape=jax.ShapeDtypeStruct((ROWS, COLS), F32),...  57.5 us
    unnamed x1, local copies, waits for them, and re-layouts  1.78 us

profile of v1, /device:TPU:6, one launch (start us, length us, event | category | flops | bytes accessed | tf_op | source)
XLA Modules:
  0.0 59.3 jit_solution(9886338513766162274)
XLA Ops:
  0.0 57.5 %couplings.1 = f32[80,1280]{1,0:T(8,128)} custom-call(s32[4096,256]{1,0:T(8,128)} %align_hbm.1, s32[32,128]{1,0:T(8,128)} %bitcast.1, f32[128,128]{1,0:T(8,128)} %inverse_ref.1), custom_call_target="tpu_custom_call" | custom-call | tf_op jit(solution)/shard_map/couplings/pallas_call | solution.py:384
  57.6 1.8 %copy.5 = f32[80,1280]{1,0:T(8,128)} copy(f32[80,1280]{1,0:T(8,128)} %couplings.1) | data formatting | bytes 819200

commit v2 on v1

v2 whole, which is shorter than its diff:
```python
import jax
import jax.numpy as jnp
from jax import lax
from jax.experimental import pallas as pl
from jax.experimental.pallas import tpu as pltpu
from jax.sharding import PartitionSpec as P

Q = 20
POS = 256
PANEL = 128
SEQS_LOCAL = 4096
ROWS = 80
COLS = 1280
MAIN = 640
LOAD = 512
LANES = 128
HOT = jnp.float8_e4m3fn
F32 = jnp.float32
MESH = pl.DeviceIdType.MESH
WIDTH = 256
CHUNKS = COLS // WIDTH
HALF = ROWS * 4
LEFT = 2 * HALF + 32
LEFT_MERGED = HALF + 32
N_COPIES = 96
HIGHEST = lax.Precision.HIGHEST
CONTRACT_LAST = (((1,), (1,)), ((), ()))


def position_of(feature):
    return (feature * 3277) >> 16


def hot_rows(state_row, value):
    lanes = LANES
    row = lax.broadcasted_iota(jnp.int32, (8, lanes), 0).astype(F32)
    parts = []
    for tile in range(Q):
        low = 8 * tile
        first, last = low // Q, (low + 7) // Q
        base = float(low - Q * first)
        states = jnp.broadcast_to(state_row(first), (8, lanes))
        level = row + base
        if last != first:
            cut = float(Q * last - low)
            before = row < cut
            states = jnp.where(before, states, jnp.broadcast_to(state_row(last), (8, lanes)))
            level = jnp.where(before, level, row - cut)
        parts.append(jnp.where(states == level, value, 0.0))
    return jnp.concatenate(parts, 0)


def kernel(
    align_hbm, sizes_ref, inverse_ref, out_ref,
    align, states, other, other_sizes, left, left_other, right, right_other,
    first, xr, pairs, yr, final, eu, er, es, mc, pc, pr, panel_cov,
    load_sem, send_sem, recv_sem,
):
    s = lax.axis_index("seq")
    r = lax.axis_index("row")
    c = lax.axis_index("col")
    yh, x = s // 4, s % 4
    x_next, x_far, x_prev = (x + 1) % 4, (x + 2) % 4, (x + 3) % 4
    odd = r % 2
    core = c % 2

    def load(i):
        rows = pl.ds(pl.multiple_of(i * LOAD, LOAD), LOAD)
        return pltpu.make_async_copy(align_hbm.at[rows, :], align.at[rows, :], load_sem.at[i])

    for i in range(SEQS_LOCAL // LOAD):
        load(i).start()

    def at_seq(dx, dy):
        return (((yh + dy) % 2) * 4 + (x + dx) % 4, r, c)

    def at_z(dz):
        return (s, (r + dz) % 8, c)

    z_mate = (s, r + 1 - 2 * odd, c)
    core_mate = (s, r, c + 1 - 2 * core)

    barrier = pltpu.get_barrier_semaphore()

    def greet(peer):
        pl.semaphore_signal(barrier, inc=1, device_id=peer, device_id_type=MESH)

    peers = [at_seq(dx, dy) for dx in range(4) for dy in range(2) if dx or dy]
    peers += [at_z(dz) for dz in (1, 2, 6, 7)]
    peers += [(s, r, (c + dc) % 4) for dc in range(1, 4)]
    for peer in peers:
        greet(peer)
    own_source = [jnp.logical_and(c == 0, s == b) for b in range(2)]
    for b in range(2):
        @pl.when(jnp.logical_not(own_source[b]))
        def _():
            greet((2 * c + b, r, 0))

    used = []
    sends = []

    def reserve(count):
        low = len(used)
        used.extend(range(low, low + count))
        return low

    def copy_at(index, src, dst, device):
        return pltpu.make_async_remote_copy(
            src_ref=src, dst_ref=dst, send_sem=send_sem.at[index], recv_sem=recv_sem.at[index],
            device_id=device, device_id_type=MESH,
        )

    def push(src, dst, device):
        copy = copy_at(reserve(1), src, dst, device)
        copy.start()
        sends.append(copy)
        return copy

    row_id = lax.broadcasted_iota(jnp.int32, (96, POS), 0)
    pos_id = lax.broadcasted_iota(jnp.int32, (96, POS), 1)
    half_id = jnp.where(row_id < 16, yh, 1 - yh)
    wanted = jnp.where(
        row_id < 32,
        half_id * 128 + ((row_id >> 2) & 3) * 32 + r * 4 + (row_id & 3),
        c * 64 + row_id - 32,
    )
    pick = (pos_id == wanted).astype(F32).astype(jnp.bfloat16)
    first_row = lax.broadcasted_iota(jnp.int32, (32, LANES), 0) == 0

    @pl.loop(0, SEQS_LOCAL // LOAD)
    def _(i):
        load(i).wait()
        span = pl.ds(pl.multiple_of(i * LOAD, LOAD), LOAD)
        block = align[span, :].astype(F32).astype(jnp.bfloat16)
        found = lax.dot_general(pick, block, CONTRACT_LAST, preferred_element_type=F32)
        for g in range(12):
            states[g, :, span] = found[8 * g:8 * g + 8]

    pl.semaphore_wait(barrier, len(peers) + jnp.where(c == 0, jnp.where(s < 2, 7, 8), 0))
    size_copy = push(sizes_ref, other_sizes, at_seq(0, 1))
    row_half = push(states.at[2 + core], other.at[core], at_seq(0, 1))
    y_base = reserve(4)
    z_base = reserve(4)

    def y_block(i):
        return 2 * i + 2 - odd

    def z_block(i):
        return 2 * i + 1 + odd

    def other_rows(b):
        return other.at[2 + b]

    def y_copy(i):
        b = y_block(i)
        return copy_at(y_base + i, states.at[4 + b], other_rows(b), at_seq(0, 1))

    def z_copy(i):
        return copy_at(z_base + i, other_rows(y_block(i)), other_rows(y_block(i)), z_mate)

    def z_arrival(i):
        return copy_at(z_base + i, other_rows(z_block(i)), other_rows(z_block(i)), z_mate)

    for i in range(3):
        y_copy(i).start()

    @pl.when(odd == 1)
    def _():
        y_copy(3).start()

    def hot_right(target, source, group, b, lanes):
        rows = pl.ds(160 * b, 160) if isinstance(b, int) else pl.ds(pl.multiple_of(160 * b, 160), 160)
        target[rows, lanes] = hot_rows(
            lambda p: source[group + b, pl.ds(p, 1), lanes], 1.0
        ).astype(HOT)

    def hot_left(target, low, source, group, blocks, weight, lanes):
        weight8 = jnp.broadcast_to(weight, (8, LANES))
        for b in range(blocks):
            target[pl.ds(low + 160 * b, 160), lanes] = hot_rows(
                lambda p: source[group + b, pl.ds(p, 1), lanes], weight8
            ).astype(HOT)

    def weight_rows(weight):
        return jnp.where(first_row, jnp.broadcast_to(weight, (32, LANES)), 0.0).astype(HOT)

    def lanes_at(i):
        return pl.ds(pl.multiple_of(i * LANES, LANES), LANES)

    @pl.loop(0, SEQS_LOCAL // LANES)
    def _(i):
        lanes = lanes_at(i)
        weight = 1.0 / sizes_ref[pl.ds(i, 1), :].astype(F32)
        hot_left(left, 0, states, 0, 2, weight, lanes)
        left[pl.ds(HALF, 32), lanes] = weight_rows(weight)
        hot_left(left, LEFT_MERGED, states, 2, 2, weight, lanes)
        for b in range(2):
            hot_right(right, states, 4, b, lanes)

    first[...] = lax.dot_general(
        left[...], right[pl.ds(0, WIDTH), :], CONTRACT_LAST, preferred_element_type=F32
    )

    def first_block(other_half, to_x):
        start = other_half * LEFT_MERGED + to_x * ROWS
        return first.at[pl.ds(pl.multiple_of(start, 8), ROWS), :]

    first_copies = [
        push(first_block(0, x_far), xr.at[0], at_seq(1, 0)),
        push(first_block(1, x_far), xr.at[1], at_seq(3, 0)),
        push(first_block(1, x_next), xr.at[2], at_seq(1, 0)),
        push(first_block(0, x_prev), xr.at[3], at_seq(3, 0)),
    ]
    @pl.loop(0, SEQS_LOCAL // LANES)
    def _(i):
        for b in range(2, 8):
            hot_right(right, states, 4, b, lanes_at(i))

    def hot_other(b):
        @pl.loop(0, SEQS_LOCAL // LANES)
        def _(i):
            hot_right(right_other, other, 2, b, lanes_at(i))

    def finish_first():
        first_copies[6].wait_recv()
        return first_block(0, x)[...] + xr[6]

    def multiply(j):
        rows = pl.ds(j * WIDTH, WIDTH)
        pairs[j - 1] = lax.dot_general(
            left[pl.ds(0, LEFT_MERGED), :], right[rows, :], CONTRACT_LAST, preferred_element_type=F32
        )

    def multiply_other(j):
        rows = pl.ds(j * WIDTH, WIDTH)
        pairs[j - 1, pl.ds(0, HALF), :] += lax.dot_general(
            left_other[...], right_other[rows, :], CONTRACT_LAST, preferred_element_type=F32
        )

    def part(j, to_x, low):
        return pairs.at[j - 1, pl.ds(pl.multiple_of(to_x * ROWS + low, 8), 40), :]

    copies = {}

    def stage_one(j):
        copies[j] = [
            push(part(j, x_far, 0), yr.at[j - 1, 0], at_seq(1, 0)),
            push(part(j, x_far, 40), yr.at[j - 1, 1], at_seq(3, 0)),
            push(part(j, x_next, 40), yr.at[j - 1, 2], at_seq(1, 0)),
            push(part(j, x_prev, 0), yr.at[j - 1, 3], at_seq(3, 0)),
        ]

    def stage_two(j):
        done = copies[j]
        done[0].wait_recv()
        part(j, x_next, 0)[...] += yr[j - 1, 0]
        done.append(push(part(j, x_next, 0), yr.at[j - 1, 4], at_seq(1, 0)))
        done[1].wait_recv()
        part(j, x_prev, 40)[...] += yr[j - 1, 1]
        done.append(push(part(j, x_prev, 40), yr.at[j - 1, 5], at_seq(3, 0)))

    def finish(j):
        for i in range(2, 6):
            copies[j][i].wait_recv()
        top = part(j, x, 0)[...] + yr[j - 1, 4] + yr[j - 1, 3]
        bottom = part(j, x, 40)[...] + yr[j - 1, 2] + yr[j - 1, 5]
        return jnp.concatenate([top, bottom], 0)

    row_half.wait_recv()
    row_share = push(other.at[core], other.at[core], core_mate)
    multiply(1)
    multiply(2)
    first_copies[0].wait_recv()
    first_block(0, x_next)[...] += xr[0]
    first_copies.append(push(first_block(0, x_next), xr.at[4], at_seq(1, 0)))
    first_copies[1].wait_recv()
    first_block(1, x_prev)[...] += xr[1]
    first_copies.append(push(first_block(1, x_prev), xr.at[5], at_seq(3, 0)))
    y_copy(0).wait_recv()
    z_copy(0).start()
    multiply(3)
    multiply(4)
    weight_sum = jnp.sum(
        jnp.sum(1.0 / sizes_ref[...].astype(F32), axis=0, keepdims=True), axis=1, keepdims=True
    )
    for tile in range(10):
        j, lanes = tile // 2, pl.ds((tile % 2) * LANES, LANES)
        eu[pl.ds(tile, 1), :] = (first if j == 0 else pairs.at[j - 1])[pl.ds(HALF, 1), lanes]
    eu[pl.ds(10, 6), :] = jnp.broadcast_to(weight_sum, (6, LANES))
    margin_sums = []
    for dx in range(4):
        for dy in range(2):
            if dx or dy:
                margin_sums.append(push(eu, er.at[dx * 2 + dy - 1], at_seq(dx, dy)))
    row_share.wait_recv()
    size_copy.wait_recv()

    @pl.loop(0, SEQS_LOCAL // LANES)
    def _(i):
        lanes = lanes_at(i)
        weight = 1.0 / other_sizes[pl.ds(i, 1), :].astype(F32)
        hot_left(left_other, 0, other, 0, 2, weight, lanes)

    for i in range(2, 6):
        first_copies[i].wait_recv()
    first_block(0, x)[...] += xr[4] + xr[3]
    first_block(1, x)[...] += xr[2] + xr[5]
    first_copies.append(push(first_block(1, x), xr.at[6], at_seq(0, 1)))
    y_copy(1).wait_recv()
    z_copy(1).start()
    hot_other(y_block(0))
    z_arrival(0).wait_recv()
    hot_other(z_block(0))
    y_copy(2).wait_recv()
    z_copy(2).start()
    hot_other(y_block(1))
    final[...] = finish_first()
    base = reserve(11)

    def panel_copy(i):
        return pltpu.make_async_remote_copy(
            src_ref=final.at[:, pl.ds(0, PANEL)], dst_ref=pc.at[s % 2, r],
            send_sem=send_sem.at[base + i], recv_sem=recv_sem.at[base + s % 2],
            device_id=(((yh + i // 4) % 2) * 4 + (x + i % 4) % 4, r, s // 2), device_id_type=MESH,
        )

    def panel_arrival(b):
        return pltpu.make_async_remote_copy(
            src_ref=final.at[:, pl.ds(0, PANEL)], dst_ref=pc.at[b, r],
            send_sem=send_sem.at[base], recv_sem=recv_sem.at[base + b],
            device_id=at_seq(1, 0), device_id_type=MESH,
        )

    def row_copy(i):
        return pltpu.make_async_remote_copy(
            src_ref=final.at[:, pl.ds(0, PANEL)], dst_ref=pr,
            send_sem=send_sem.at[base + 8 + i], recv_sem=recv_sem.at[base + 8],
            device_id=(s, r, (c + 1 + i) % 4), device_id_type=MESH,
        )

    sends_panel = c == 0
    to_itself = jnp.logical_and(sends_panel, s < 2)
    to_another = jnp.logical_and(sends_panel, s >= 2)

    @pl.when(sends_panel)
    def _():
        for i in range(1, 8):
            panel_copy(i).start()

    @pl.when(to_another)
    def _():
        panel_copy(0).start()

    @pl.when(to_itself)
    def _():
        pc[s % 2, r] = final[:, pl.ds(0, PANEL)]

    @pl.when(sends_panel)
    def _():
        for i in range(3):
            row_copy(i).start()
        pr[...] = final[:, pl.ds(0, PANEL)]

    z_arrival(1).wait_recv()
    hot_other(z_block(1))

    @pl.when(odd == 1)
    def _():
        y_copy(3).wait_recv()
        z_copy(3).start()

    multiply_other(1)
    stage_one(1)
    multiply_other(2)
    stage_one(2)
    hot_other(y_block(2))
    z_arrival(2).wait_recv()
    hot_other(z_block(2))
    stage_two(1)
    multiply_other(3)
    stage_one(3)

    total = eu[...]
    for i in range(7):
        margin_sums[i].wait_recv()
        total = total + er[i]
    es[...] = total
    mc[c] = total
    margin_gathers = [push(es, mc.at[c], (s, r, (c + dc) % 4)) for dc in range(1, 4)]
    for b in range(2):
        @pl.when(jnp.logical_not(own_source[b]))
        def _():
            panel_arrival(b).wait_recv()

    z_copies = [push(pc.at[:, r], pc.at[:, r], at_z(dz)) for dz in (2, 6, 1, 7)]
    @pl.when(odd == 0)
    def _():
        z_arrival(3).wait_recv()

    hot_other(7)
    stage_two(2)
    multiply_other(4)
    stage_one(4)
    stage_two(3)
    low_z, high_z = (r + 6) % 8, (r + 2) % 8
    z_copies[0].wait_recv()
    z_copies.append(push(pc.at[:, low_z], pc.at[:, low_z], at_z(1)))
    z_copies.append(push(pc.at[0, low_z], pc.at[0, low_z], at_z(2)))
    z_copies[1].wait_recv()
    z_copies.append(push(pc.at[:, high_z], pc.at[:, high_z], at_z(7)))
    z_copies.append(push(pc.at[1, high_z], pc.at[1, high_z], at_z(6)))

    @pl.when(c != 0)
    def _():
        row_copy(0).wait_recv()

    for copy in margin_gathers:
        copy.wait_recv()
    half = 0.5 / mc[c, pl.ds(10, 1), :]
    floor = 0.5 / Q
    half_cols = jnp.concatenate([half] * 10, 1)
    col_freq = (
        jnp.concatenate([mc[c, pl.ds(i, 1), :] for i in range(10)], 1) * half_cols + floor
    )
    panel_freq = mc[0, pl.ds(0, 1), :] * half + floor
    row_low = (s * 8 + r) * ROWS
    local = (s % 2) * MAIN + r * ROWS + lax.broadcasted_iota(jnp.int32, (ROWS, LANES), 0)
    lane = lax.broadcasted_iota(jnp.int32, (ROWS, LANES), 1)
    found = jnp.zeros((ROWS, LANES), F32)
    for i in range(10):
        margin = jnp.broadcast_to(mc[s // 2, pl.ds(i, 1), :] * half, (ROWS, LANES))
        found += jnp.where(local == lane + i * LANES, margin, 0.0)
    row_freq = jnp.sum(found, axis=1, keepdims=True) + floor
    eye = lax.broadcasted_iota(jnp.int32, (PANEL, PANEL), 0) == lax.broadcasted_iota(
        jnp.int32, (PANEL, PANEL), 1
    )

    def prior(shape, row_first, col_first):
        row = row_first + lax.broadcasted_iota(jnp.int32, shape, 0)
        col = col_first + lax.broadcasted_iota(jnp.int32, shape, 1)
        return jnp.where(
            position_of(row) == position_of(col),
            jnp.where(row == col, 0.5 / Q, 0.0),
            0.5 / (Q * Q),
        )

    panel_rows = pr[...] * half + prior((ROWS, PANEL), row_low, 0) - row_freq * panel_freq
    symmetric = 0.5 * (inverse_ref[...] + inverse_ref[...].T)
    factor = jnp.dot(panel_rows, symmetric, precision=HIGHEST, preferred_element_type=F32)
    for i in range(10):
        lanes = slice(i * LANES, (i + 1) * LANES)
        freq = jnp.broadcast_to(col_freq[:, lanes], (PANEL, PANEL))
        column = jnp.sum(jnp.where(eye, freq, 0.0), axis=1, keepdims=True)
        panel_cov[pl.ds(i * LANES, LANES), :] = (
            prior((PANEL, PANEL), c * COLS + i * LANES, 0) - column * panel_freq
        )
    for j in range(CHUNKS):
        low, width = j * WIDTH, WIDTH
        shift = prior((ROWS, width), row_low, c * COLS + low)
        shift = shift - row_freq * col_freq[:, low:low + width]
        out_ref[:, pl.ds(low, width)] = -float(Q) * shift
    stage_two(4)
    for copy in z_copies[2:]:
        copy.wait_recv()
    for b in range(2):
        for z in range(8):
            panel_cov[pl.ds((b * 8 + z) * ROWS, ROWS), :] += pc[b, z] * half
    for j in range(CHUNKS):
        low, width = j * WIDTH, WIDTH
        update = lax.dot_general(
            factor, panel_cov[pl.ds(low, width), :], CONTRACT_LAST, precision=HIGHEST,
            preferred_element_type=F32,
        )
        out_ref[:, pl.ds(low, width)] += float(Q) * update
    for j in range(CHUNKS):
        low, width = j * WIDTH, WIDTH
        sums = final[...] if j == 0 else finish(j)
        out_ref[:, pl.ds(low, width)] += sums * (half_cols[:, low:low + width] * -float(Q))

    for copy in sends:
        copy.wait_send()
    for i in range(3):
        y_copy(i).wait_send()
        z_copy(i).wait_send()

    @pl.when(odd == 1)
    def _():
        y_copy(3).wait_send()
        z_copy(3).wait_send()

    @pl.when(sends_panel)
    def _():
        for i in range(1, 8):
            panel_copy(i).wait_send()
        for i in range(3):
            row_copy(i).wait_send()

    @pl.when(to_another)
    def _():
        panel_copy(0).wait_send()

    assert len(used) <= N_COPIES


def shards(alignment, cluster_sizes, block_inverse):
    vmem = pl.BlockSpec(memory_space=pltpu.VMEM)

    return pl.pallas_call(
        kernel,
        out_shape=jax.ShapeDtypeStruct((ROWS, COLS), F32),
        in_specs=[pl.BlockSpec(memory_space=pl.ANY), vmem, vmem],
        out_specs=vmem,
        scratch_shapes=[
            pltpu.VMEM((SEQS_LOCAL, POS), jnp.int32),
            pltpu.VMEM((12, 8, SEQS_LOCAL), F32),
            pltpu.VMEM((10, 8, SEQS_LOCAL), F32),
            pltpu.VMEM((SEQS_LOCAL // LANES, LANES), jnp.int32),
            pltpu.VMEM((LEFT, SEQS_LOCAL), HOT),
            pltpu.VMEM((HALF, SEQS_LOCAL), HOT),
            pltpu.VMEM((COLS, SEQS_LOCAL), HOT),
            pltpu.VMEM((COLS, SEQS_LOCAL), HOT),
            pltpu.VMEM((LEFT, WIDTH), F32),
            pltpu.VMEM((7, ROWS, WIDTH), F32),
            pltpu.VMEM((CHUNKS - 1, LEFT_MERGED, WIDTH), F32),
            pltpu.VMEM((CHUNKS - 1, 6, 40, WIDTH), F32),
            pltpu.VMEM((ROWS, WIDTH), F32),
            pltpu.VMEM((16, LANES), F32),
            pltpu.VMEM((7, 16, LANES), F32),
            pltpu.VMEM((16, LANES), F32),
            pltpu.VMEM((4, 16, LANES), F32),
            pltpu.VMEM((2, 8, ROWS, PANEL), F32),
            pltpu.VMEM((ROWS, PANEL), F32),
            pltpu.VMEM((COLS, PANEL), F32),
            pltpu.SemaphoreType.DMA((SEQS_LOCAL // LOAD,)),
            pltpu.SemaphoreType.DMA((N_COPIES,)),
            pltpu.SemaphoreType.DMA((N_COPIES,)),
        ],
        compiler_params=pltpu.CompilerParams(
            collective_id=0, has_side_effects=True, vmem_limit_bytes=56 * 2**20
        ),
        name="couplings",
    )(alignment, cluster_sizes.reshape(SEQS_LOCAL // LANES, LANES), block_inverse)


def solution(mesh):
    in_specs = (P("seq", None), P("seq"), P())
    out_specs = P(("seq", "row"), "col")
    return jax.shard_map(shards, mesh=mesh, in_specs=in_specs, out_specs=out_specs, check_vma=False)
```

time: 60.3 us -> 51.5 us (0.85)
  Pallas kernels: 57.5 us -> 48.8 us
    pallas_call x1, Pallas kernels: 57.5 us -> 48.8 us  [shards(): pl.pallas_call(kernel, out_shape=jax.ShapeDtypeStruct((ROWS, COLS), F32),...]
where the time goes in v2:
time: 51.5 us; the launch traced here: 50.6 us
  Pallas kernels  48.8 us (95%)
  local copies, waits for them, and re-layouts  1.78 us (3%)
    pallas_call x1, Pallas kernels, shards(): pl.pallas_call(kernel, out_shape=jax.ShapeDtypeStruct((ROWS, COLS), F32),...  48.8 us
    unnamed x1, local copies, waits for them, and re-layouts  1.78 us

profile of v2, /device:TPU:6, one launch (start us, length us, event | category | flops | bytes accessed | tf_op | source)
XLA Modules:
  0.0 50.6 jit_solution(3345623113764119326)
XLA Ops:
  0.0 48.8 %couplings.1 = f32[80,1280]{1,0:T(8,128)} custom-call(s32[4096,256]{1,0:T(8,128)} %align_hbm.1, s32[32,128]{1,0:T(8,128)} %bitcast.1, f32[128,128]{1,0:T(8,128)} %inverse_ref.1), custom_call_target="tpu_custom_call" | custom-call | tf_op jit(solution)/shard_map/couplings/pallas_call | solution.py:508
  48.8 1.8 %copy.5 = f32[80,1280]{1,0:T(8,128)} copy(f32[80,1280]{1,0:T(8,128)} %couplings.1) | data formatting | bytes 819200

commit v3 on v2

--- a/solution.py
+++ b/solution.py
@@ -460,6 +460,12 @@
         shift = shift - row_freq * col_freq[:, low:low + width]
         out_ref[:, pl.ds(low, width)] = -float(Q) * shift
     stage_two(4)
+    def halves(value):
+        high = value.astype(jnp.bfloat16)
+        return high, (value - high.astype(F32)).astype(jnp.bfloat16)
+
+    factor_high, factor_low = halves(factor)
+    factor_parts = jnp.concatenate([factor_high, factor_low, factor_high], 1)
     for copy in z_copies[2:]:
         copy.wait_recv()
     for b in range(2):
@@ -467,8 +473,9 @@
             panel_cov[pl.ds((b * 8 + z) * ROWS, ROWS), :] += pc[b, z] * half
     for j in range(CHUNKS):
         low, width = j * WIDTH, WIDTH
+        high, low_part = halves(panel_cov[pl.ds(low, width), :])
         update = lax.dot_general(
-            factor, panel_cov[pl.ds(low, width), :], CONTRACT_LAST, precision=HIGHEST,
+            factor_parts, jnp.concatenate([high, high, low_part], 1), CONTRACT_LAST,
             preferred_element_type=F32,
         )
         out_ref[:, pl.ds(low, width)] += float(Q) * update

time: 51.5 us -> 51.2 us (level)
  no operation moved by 1% of the time
where the time goes in v3:
time: 51.2 us; the launch traced here: 50.2 us
  Pallas kernels  48.4 us (95%)
  local copies, waits for them, and re-layouts  1.78 us (3%)
    pallas_call x1, Pallas kernels, shards(): pl.pallas_call(kernel, out_shape=jax.ShapeDtypeStruct((ROWS, COLS), F32),...  48.4 us
    unnamed x1, local copies, waits for them, and re-layouts  1.78 us

profile of v3, /device:TPU:6, one launch (start us, length us, event | category | flops | bytes accessed | tf_op | source)
XLA Modules:
  0.0 50.2 jit_solution(10398117668101905418)
XLA Ops:
  0.0 48.4 %couplings.1 = f32[80,1280]{1,0:T(8,128)} custom-call(s32[4096,256]{1,0:T(8,128)} %align_hbm.1, s32[32,128]{1,0:T(8,128)} %bitcast.1, f32[128,128]{1,0:T(8,128)} %inverse_ref.1), custom_call_target="tpu_custom_call" | custom-call | tf_op jit(solution)/shard_map/couplings/pallas_call | solution.py:515
  48.4 1.8 %copy.5 = f32[80,1280]{1,0:T(8,128)} copy(f32[80,1280]{1,0:T(8,128)} %couplings.1) | data formatting | bytes 819200
